TPU v7x, 256 devices: a whole 4x4x8 slice. The times are simulated.
256 devices in a mesh: seq: 64 (over y, z, core), chan: 4 (over x).
Axes of the slice: x: 4, y: 4, z: 8, core: 2. Of those that a mesh axis runs over, the one named last changes fastest.
Arguments:
- inputs: bfloat16 [32768, 1536], P('seq', 'chan'), may hold values from -16 to 16
- conv_weight: bfloat16 [1, 3, 1536, 1536], P(None, None, None, 'chan'), may hold values from -0.09375 to 0.09375
- head_weight: bfloat16 [1536, 4096], P(None, 'chan'), may hold values from -0.15625 to 0.15625
- head_cot: bfloat16 [32768, 4096], P('seq', 'chan'), may hold values from -6 to 6
- exon_blocks: int32 [512, 8], P('seq'), may hold values from 0 to 255
Outputs:
- tracks: bfloat16 [32768, 4096], P('seq', 'chan')
- coverage: float32 [512, 4096], P('seq', 'chan')
- input_grad: bfloat16 [32768, 1536], P('seq', 'chan')
- kernel_gradient: float32 [1, 3, 1536, 1536], P(None, None, 'seq', 'chan')
All inputs are finite; a program needn't handle non-finite values.
Results may differ from a plain program's by a relative error of at most 0.0059.
Values may be sent and summed in bfloat16 or wider, within the bound.
No kernel may reach another device: no remote copies, remote signals or barrier semaphores. Data moves between devices by JAX's collectives and lax.ppermute only.
A program may use at most 64 MiB of HBM per device.

v0:
```python
import jax
import jax.numpy as jnp
from jax import lax
from jax.sharding import PartitionSpec as P

BLOCK = 128
EXONS = 8


def shifted(value, axis, steps):
    count = lax.axis_size(axis)
    leading, last = (max(0, -steps), min(count, count - steps))
    return lax.ppermute(value, axis, [(source, source + steps) for source in range(leading, last)])


def activation_slope(point, cotan):
    _, back = jax.vjp(jax.nn.gelu, point)
    return back(cotan)[0]


def tap_input(values, steps):
    return shifted(values, "seq", steps)


def tap_grad(values, steps):
    return shifted(values, "seq", steps)


def times_t(left, right):
    return lax.dot_general(
        left, right, (((1,), (1,)), ((), ())), preferred_element_type=jnp.float32
    )


def inner_rows(left, right):
    return lax.dot_general(
        left, right, (((0,), (0,)), ((), ())), preferred_element_type=jnp.float32
    )


def shards(inputs, conv_weight, head_weight, head_cot, exon_blocks):
    rows = inputs.shape[0]
    state = inputs
    layer_number = 0
    steps = 2 * 2**layer_number
    acted = jax.nn.gelu(state.astype(jnp.float32)).astype(jnp.bfloat16)
    lower = tap_input(acted, steps)
    upper = tap_input(acted, -steps)
    whole = lax.all_gather(acted, "chan", axis=1, tiled=True)
    whole_low = lax.all_gather(lower, "chan", axis=1, tiled=True)
    whole_up = lax.all_gather(upper, "chan", axis=1, tiled=True)
    mixed = jnp.dot(whole_low, conv_weight[layer_number, 0], preferred_element_type=jnp.float32)
    mixed = mixed + jnp.dot(whole, conv_weight[layer_number, 1], preferred_element_type=jnp.float32)
    mixed = mixed + jnp.dot(
        whole_up, conv_weight[layer_number, 2], preferred_element_type=jnp.float32
    )
    saved = [(state, whole, steps)]
    state = (state.astype(jnp.float32) + mixed).astype(jnp.bfloat16)
    full_state = lax.all_gather(state, "chan", axis=1, tiled=True)
    logits = jnp.dot(full_state, head_weight, preferred_element_type=jnp.float32)
    tracks = jax.nn.softplus(logits).astype(jnp.bfloat16)
    head_term = (head_cot.astype(jnp.float32) * jax.nn.sigmoid(logits)).astype(jnp.bfloat16)
    grad = lax.psum_scatter(
        times_t(head_term, head_weight), "chan", scatter_dimension=1, tiled=True
    )
    grads = []
    for layer_number in reversed(range(conv_weight.shape[0])):
        before, whole, steps = saved[layer_number]
        grad_low = grad.astype(jnp.bfloat16)
        later = tap_grad(grad_low, -steps)
        earlier = tap_grad(grad_low, steps)
        partial_value = times_t(later, conv_weight[layer_number, 0])
        partial_value = partial_value + times_t(grad_low, conv_weight[layer_number, 1])
        partial_value = partial_value + times_t(earlier, conv_weight[layer_number, 2])
        back_u = lax.psum_scatter(partial_value, "chan", scatter_dimension=1, tiled=True)
        kernel = jnp.stack(
            [inner_rows(whole, later), inner_rows(whole, grad_low), inner_rows(whole, earlier)]
        )
        grads.append(lax.psum_scatter(kernel, "seq", scatter_dimension=1, tiled=True))
        grad = grad + activation_slope(before.astype(jnp.float32), back_u)
    kernel_gradient = jnp.stack(grads[::-1])
    resident_blocks = rows // BLOCK
    block_partial_sums = (
        tracks.astype(jnp.float32).reshape(resident_blocks, BLOCK, tracks.shape[1]).sum(axis=1)
    )
    scale = jnp.sqrt(jnp.float32(EXONS * BLOCK))
    all_blocks = lax.all_gather(block_partial_sums, "seq", axis=0, tiled=True)
    labels = jnp.arange(all_blocks.shape[0], dtype=jnp.int32)
    counts = jnp.sum((exon_blocks[:, :, None] == labels[None, None, :]).astype(jnp.float32), axis=1)
    coverage = jnp.dot(counts, all_blocks, precision=lax.Precision.HIGHEST) / scale
    return (tracks, coverage, grad.astype(jnp.bfloat16), kernel_gradient)


def solution(mesh):
    return jax.shard_map(
        shards,
        mesh=mesh,
        in_specs=(
            P("seq", "chan"),
            P(None, None, None, "chan"),
            P(None, "chan"),
            P("seq", "chan"),
            P("seq", None),
        ),
        out_specs=(
            P("seq", "chan"),
            P("seq", "chan"),
            P("seq", "chan"),
            P(None, None, "seq", "chan"),
        ),
        check_vma=False,
    )
```

profile of v0, /device:TPU:2, one launch (start us, length us, event | category | flops | bytes accessed | tf_op | source)
XLA Modules:
  0.0 468.9 jit_solution(14514463337364591084)
XLA Ops:
  7.2 0.0 copy-start
  7.2 0.0 all-gather.9.cloned.1.call-start
  7.2 2.2 fusion.30
  9.4 0.0 all-gather.9.cloned.1.call-update
  9.4 0.0 all-gather.11.cloned.1.call-start
  9.5 1.3 collective-permute-start.1
  10.8 11.8 %collective-permute-done.1 = bf16[512,384]{1,0:T(8,128)(2,1)S(1)} collective-permute-done((bf16[512,384]{1,0:T(8,128)(2,1)}, bf16[512,384]{1,0:T(8,128)(2,1)S(1)}, u32[]{:S(2)}, u32[]{:S(2)}) %collective-permute-start.1) | collective-permute-done | bytes 393248 | tf_op jit(solution)/shard_map/ppermute | solution.py:13
  22.6 0.7 copy-done.8
  23.4 0.0 all-gather.11.cloned.1.call-update
  23.4 0.0 all-gather.7.cloned.1.call-start
  23.4 3.8 collective-permute-start
  27.3 8.0 %collective-permute-done = bf16[512,384]{1,0:T(8,128)(2,1)S(1)} collective-permute-done((bf16[512,384]{1,0:T(8,128)(2,1)}, bf16[512,384]{1,0:T(8,128)(2,1)S(1)}, u32[]{:S(2)}, u32[]{:S(2)}) %collective-permute-start) | collective-permute-done | bytes 393248 | tf_op jit(solution)/shard_map/ppermute | solution.py:13
  35.3 0.7 copy-done.9
  36.0 0.0 all-gather.7.cloned.1.call-update
  36.0 0.0 all-gather.13.cloned.1.call-start
  36.1 5.5 %all-gather.9.cloned.1.call-done = bf16[512,1536]{1,0:T(8,128)(2,1)} async-done(((bf16[512,384]{1,0:T(8,128)(2,1)}), bf16[512,1536]{1,0:T(8,128)(2,1)}) %all-gather.9.cloned.1.call-update) | async-done | bytes 1572880 | tf_op jit(solution)/shard_map/all_gather | solution.py:49
  41.5 3.6 fusion.10
  45.2 27.9 %all-gather.11.cloned.1.call-done = bf16[512,1536]{1,0:T(8,128)(2,1)} async-done(((bf16[512,384]{1,0:T(8,128)(2,1)}), bf16[512,1536]{1,0:T(8,128)(2,1)}) %all-gather.11.cloned.1.call-update) | async-done | bytes 1572880 | tf_op jit(solution)/shard_map/all_gather | solution.py:51
  73.1 3.6 fusion.6
  76.7 27.4 %all-gather.7.cloned.1.call-done = bf16[512,1536]{1,0:T(8,128)(2,1)} async-done(((bf16[512,384]{1,0:T(8,128)(2,1)}), bf16[512,1536]{1,0:T(8,128)(2,1)}) %all-gather.7.cloned.1.call-update) | async-done | bytes 1572880 | tf_op jit(solution)/shard_map/all_gather | solution.py:50
  104.1 0.0 copy-done.2
  104.1 3.9 fusion.3
  108.1 0.0 all-gather.13.cloned.1.call-update
  108.1 0.0 reduce-scatter.4.cloned.1.call-start
  108.1 29.2 %all-gather.13.cloned.1.call-done = bf16[512,1536]{1,0:T(8,128)(2,1)} async-done(((bf16[512,384]{1,0:T(8,128)(2,1)}), bf16[512,1536]{1,0:T(8,128)(2,1)}) %all-gather.13.cloned.1.call-update) | async-done | bytes 1572880 | tf_op jit(solution)/shard_map/all_gather | solution.py:59
  137.4 0.0 copy-done
  137.4 5.8 %convert_reduce_fusion = (f32[4,1024]{1,0:T(4,128)}, bf16[512,1024]{1,0:T(8,128)(2,1)}, f32[512,1024]{1,0:T(8,128)S(1)}) fusion(bf16[512,1536]{1,0:T(8,128)(2,1)} %all-gather.13.cloned.1.call-done, bf16[1536,1024]{1,0:T(8,128)(2,1)S(1)} %copy-done), kind=kOutput, calls=%fused_computation.8 | convolution fusion | flops 1615327232 | bytes 7880704 | tf_op jit(solution)/shard_map/dot_general | solution.py:60
  143.2 0.0 copy-done.12
  143.2 3.5 fusion.15
  146.7 0.0 reduce-scatter.4.cloned.1.call-update
  146.7 0.0 all-gather.15.cloned.1.call-start
  146.8 0.5 all-gather.15.cloned.1.call-update
  147.3 0.0 reduce-scatter.6.cloned.1.call-start
  147.3 40.1 %reduce-scatter.4.cloned.1.call-done = f32[512,384]{1,0:T(8,128)} async-done(((f32[512,1536]{1,0:T(8,128)}), f32[512,384]{1,0:T(8,128)}) %reduce-scatter.4.cloned.1.call-update) | async-done | bytes 786448 | tf_op jit(solution)/shard_map/reduce_scatter | solution.py:63
  187.4 1.2 convert_element_type.37
  188.6 0.0 copy-start.3
  188.6 0.0 copy-start.1
  188.6 3.7 collective-permute-start.3
  192.4 1.3 collective-permute-start.2
  193.7 2.3 fusion.8
  196.0 0.0 copy-done.3
  196.0 4.8 %collective-permute-done.3 = bf16[512,384]{1,0:T(8,128)(2,1)S(1)} collective-permute-done((bf16[512,384]{1,0:T(8,128)(2,1)S(1)}, bf16[512,384]{1,0:T(8,128)(2,1)S(1)}, u32[]{:S(2)}, u32[]{:S(2)}) %collective-permute-start.3) | collective-permute-done | bytes 393248 | tf_op jit(solution)/shard_map/ppermute | solution.py:13
  200.8 0.0 copy-done.1
  200.8 1.0 fusion.4
  201.8 3.1 collective-permute-done.2
  204.9 0.7 copy-done.4
  205.6 2.7 fusion
  208.4 0.0 reduce-scatter.6.cloned.1.call-update
  208.4 0.2 reduce-scatter.8.cloned.1.call-start
  208.6 0.0 copy-start.7
  208.6 2.6 convolution_bitcast_fusion.1
  211.3 0.0 copy-done.7
  211.3 1.0 convolution_bitcast_fusion
  212.3 1.0 convolution_bitcast_fusion.2
  213.3 3.3 pad_maximum_fusion
  216.7 0.0 reduce-scatter.8.cloned.1.call-update
  216.7 0.7 copy-done.10
  217.4 0.1 convert_reduce_fusion.1
  217.4 50.6 %all-gather.15.cloned.1.call-done = f32[64,4,1024]{2,1,0:T(4,128)} async-done(((f32[1,4,1024]{2,1,0:T(4,128)}), f32[64,4,1024]{2,1,0:T(4,128)}) %all-gather.15.cloned.1.call-update) | async-done | bytes 1048592 | tf_op jit(solution)/shard_map/all_gather | solution.py:87
  268.0 2.6 reshape.20
  270.6 2.4 convolution_multiply_fusion
  273.1 34.8 %reduce-scatter.6.cloned.1.call-done = f32[512,384]{1,0:T(8,128)} async-done(((f32[512,1536]{1,0:T(8,128)}), f32[512,384]{1,0:T(8,128)}) %reduce-scatter.6.cloned.1.call-update) | async-done | bytes 786448 | tf_op jit(solution)/shard_map/reduce_scatter | solution.py:75
  307.9 2.7 fusion.26
  310.6 151.5 %reduce-scatter.8.cloned.1.call-done = f32[3,24,384]{2,1,0:T(8,128)} async-done(((f32[3,1536,384]{2,1,0:T(8,128)}), f32[3,24,384]{2,1,0:T(8,128)}) %reduce-scatter.8.cloned.1.call-update) | async-done | bytes 110608 | tf_op jit(solution)/shard_map/reduce_scatter | solution.py:79
  (12 shorter events, 0.0 us)
Async XLA Ops:
  7.2 130.2 %copy-start = (bf16[1536,1024]{1,0:T(8,128)(2,1)S(1)}, bf16[1536,1024]{1,0:T(8,128)(2,1)}, u32[]{:S(2)}) copy-start(bf16[1536,1024]{1,0:T(8,128)(2,1)} %param.7) | copy-start | bytes 9437188
  7.2 34.4 %all-gather.9.cloned.1.call-start = ((), (), s32[]{:S(2)}) async-start(), calls=%async_computation.4 | async-start | bytes 1966080 | tf_op jit(solution)/shard_map/all_gather | solution.py:49
  9.4 63.7 %all-gather.11.cloned.1.call-start = ((), (), s32[]{:S(2)}) async-start(), calls=%async_computation.5 | async-start | bytes 1966080 | tf_op jit(solution)/shard_map/all_gather | solution.py:51
  9.5 13.1 %collective-permute-start.1 = (bf16[512,384]{1,0:T(8,128)(2,1)}, bf16[512,384]{1,0:T(8,128)(2,1)S(1)}, u32[]{:S(2)}, u32[]{:S(2)}) collective-permute-start(bf16[512,384]{1,0:T(8,128)(2,1)} %fusion.30), channel_id=1, source_target_pairs={{8,0},{12,4},{16,8},{20,12},{24,16},{28,20},{32,24},{36,28},{40,32... | collective-permute-start | bytes 1179656 | tf_op jit(solution)/shard_map/ppermute | solution.py:13
  22.6 0.7 copy-start.8
  23.4 80.7 %all-gather.7.cloned.1.call-start = ((), (), s32[]{:S(2)}) async-start(), calls=%async_computation.3 | async-start | bytes 1966080 | tf_op jit(solution)/shard_map/all_gather | solution.py:50
  23.4 11.8 %collective-permute-start = (bf16[512,384]{1,0:T(8,128)(2,1)}, bf16[512,384]{1,0:T(8,128)(2,1)S(1)}, u32[]{:S(2)}, u32[]{:S(2)}) collective-permute-start(bf16[512,384]{1,0:T(8,128)(2,1)} %fusion.30), channel_id=1, source_target_pairs={{0,8},{4,12},{8,16},{12,20},{16,24},{20,28},{24,32},{28,36},{32,40... | collective-permute-start | bytes 1179656 | tf_op jit(solution)/shard_map/ppermute | solution.py:13
  35.3 0.7 copy-start.9
  36.0 101.3 %all-gather.13.cloned.1.call-start = ((), (), s32[]{:S(2)}) async-start(), calls=%async_computation.6 | async-start | bytes 1966080 | tf_op jit(solution)/shard_map/all_gather | solution.py:59
  45.2 59.0 %copy-start.2 = (bf16[512,384]{1,0:T(8,128)(2,1)S(1)}, bf16[512,384]{1,0:T(8,128)(2,1)}, u32[]{:S(2)}) copy-start(bf16[512,384]{1,0:T(8,128)(2,1)} %param.5) | copy-start | bytes 1179652
  108.1 79.3 %reduce-scatter.4.cloned.1.call-start = ((), (), s32[]{:S(2)}) async-start(), calls=%async_computation.7 | async-start | bytes 3932160 | tf_op jit(solution)/shard_map/reduce_scatter | solution.py:63
  137.4 5.8 %copy-start.12 = (bf16[512,1024]{1,0:T(8,128)(2,1)S(1)}, bf16[512,1024]{1,0:T(8,128)(2,1)}, u32[]{:S(2)}) copy-start(bf16[512,1024]{1,0:T(8,128)(2,1)} %param.8) | copy-start | bytes 3145732
  146.7 121.3 %all-gather.15.cloned.1.call-start = ((), (), s32[]{:S(2)}) async-start(), calls=%async_computation.10 | async-start | bytes 1064960 | tf_op jit(solution)/shard_map/all_gather | solution.py:87
  147.3 160.6 %reduce-scatter.6.cloned.1.call-start = ((), (), s32[]{:S(2)}) async-start(), calls=%async_computation.8 | async-start | bytes 3932160 | tf_op jit(solution)/shard_map/reduce_scatter | solution.py:75
  188.6 7.4 %copy-start.3 = (bf16[512,384]{1,0:T(8,128)(2,1)}, bf16[512,384]{1,0:T(8,128)(2,1)S(1)}, u32[]{:S(2)}) copy-start(bf16[512,384]{1,0:T(8,128)(2,1)S(1)} %convert_element_type.37) | copy-start | bytes 1179652
  188.6 12.1 %copy-start.1 = (bf16[1,3,1536,384]{3,2,1,0:T(8,128)(2,1)S(1)}, bf16[1,3,1536,384]{3,2,1,0:T(8,128)(2,1)}, u32[]{:S(2)}) copy-start(bf16[1,3,1536,384]{3,2,1,0:T(8,128)(2,1)} %param.6) | copy-start | bytes 10616836
  188.6 12.1 %collective-permute-start.3 = (bf16[512,384]{1,0:T(8,128)(2,1)S(1)}, bf16[512,384]{1,0:T(8,128)(2,1)S(1)}, u32[]{:S(2)}, u32[]{:S(2)}) collective-permute-start(bf16[512,384]{1,0:T(8,128)(2,1)S(1)} %convert_element_type.37), channel_id=1, source_target_pairs={{0,8},{4,12},{8,16},{12,20},{16,24},{20,28},{24,32},{28,36},{32,40... | collective-permute-start | bytes 1179656 | tf_op jit(solution)/shard_map/ppermute | solution.py:13
  192.4 12.5 %collective-permute-start.2 = (bf16[512,384]{1,0:T(8,128)(2,1)S(1)}, bf16[512,384]{1,0:T(8,128)(2,1)S(1)}, u32[]{:S(2)}, u32[]{:S(2)}) collective-permute-start(bf16[512,384]{1,0:T(8,128)(2,1)S(1)} %convert_element_type.37), channel_id=1, source_target_pairs={{8,0},{12,4},{16,8},{20,12},{24,16},{28,20},{32,24},{36,28},{40,32... | collective-permute-start | bytes 1179656 | tf_op jit(solution)/shard_map/ppermute | solution.py:13
  200.8 1.0 copy-start.6
  204.9 0.7 copy-start.4
  208.4 253.7 %reduce-scatter.8.cloned.1.call-start = ((), (), s32[]{:S(2)}) async-start(), calls=%async_computation.9 | async-start | bytes 7188480 | tf_op jit(solution)/shard_map/reduce_scatter | solution.py:79
  208.6 2.7 copy-start.7
  208.6 2.6 copy-start.11
  211.3 1.0 copy-start.5
  216.7 0.7 copy-start.10
Sparse Core Ops, SparseCore 0:
  10.4 31.0 all-gather.8
  44.0 29.1 all-gather.10
  75.0 29.1 all-gather.6
  108.2 29.1 all-gather.12
  146.8 40.5 reduce-scatter.3
  190.6 77.3 all-gather.14
  270.6 37.2 reduce-scatter.5
  312.7 149.2 reduce-scatter.7
where the time goes:
time: 469 us
  waiting for transfers between devices  395 us (84%)
  matrix products  33.6 us (7%)
  between operations  14.3 us (3%)
  starting transfers between devices  10.7 us (2%)
  other arithmetic  9.47 us (2%)
  local copies, waits for them, and re-layouts  5.52 us (1%)
    reduce_scatter x1, waiting for transfers between devices, shards(): lax.psum_scatter(kernel, 'seq', scatter_dimension=1, tiled=True)  151 us
    all_gather x1, waiting for transfers between devices, shards(): all_blocks = lax.all_gather(block_partial_sums, 'seq', axis=0, tiled=True)  50.6 us
    reduce_scatter x1, waiting for transfers between devices, shards(): lax.psum_scatter(times_t(head_term, head_weight), 'chan', scatter_dimensi...  40.1 us
    reduce_scatter x1, waiting for transfers between devices, shards(): lax.psum_scatter(partial_value, 'chan', scatter_dimension=1, tiled=True)  34.8 us
    all_gather x1, waiting for transfers between devices, shards(): full_state = lax.all_gather(state, 'chan', axis=1, tiled=True)  29.2 us
    all_gather x1, waiting for transfers between devices, shards(): whole_up = lax.all_gather(upper, 'chan', axis=1, tiled=True)  27.9 us
    ppermute x4, waiting for transfers between devices, shifted(): lax.ppermute(value, axis, [(source, source + steps) for source in range(l...  27.7 us
    all_gather x1, waiting for transfers between devices, shards(): whole_low = lax.all_gather(lower, 'chan', axis=1, tiled=True)  27.4 us
  transfers between devices with their start and end apart: 12, of which 12 were waited for; matrix products, arithmetic and copies ran while one was open for 6% of the time, Pallas kernels for 0%

commit v1 on v0

--- a/solution.py
+++ b/solution.py
@@ -1,3 +1,4 @@
+import functools
 import jax
 import jax.numpy as jnp
 from jax import lax
@@ -5,6 +6,25 @@
 
 BLOCK = 128
 EXONS = 8
+
+
+def rest_works(chunk, along_axis):
+    block_list = [chunk]
+    world = jax.lax.axis_size(along_axis)
+    it = 0
+    while it < world - 1:
+        known = jax.lax.ppermute(
+            block_list[-1], along_axis, [(no, (no + 1) % world) for no in range(world)]
+        )
+        block_list.append(known)
+        it = it + 1
+    z2 = jnp.concatenate(block_list[::-1], 1)
+    small = jax.lax.axis_index(along_axis)
+    met_up = jnp.roll(z2, (small + 1) * chunk.shape[1], axis=1)
+    return met_up
+
+
+store_state = functools.partial(rest_works, along_axis="chan")
 
 
 def shifted(value, axis, steps):
@@ -48,7 +68,7 @@
     upper = tap_input(acted, -steps)
     whole = lax.all_gather(acted, "chan", axis=1, tiled=True)
     whole_low = lax.all_gather(lower, "chan", axis=1, tiled=True)
-    whole_up = lax.all_gather(upper, "chan", axis=1, tiled=True)
+    whole_up = store_state(upper)
     mixed = jnp.dot(whole_low, conv_weight[layer_number, 0], preferred_element_type=jnp.float32)
     mixed = mixed + jnp.dot(whole, conv_weight[layer_number, 1], preferred_element_type=jnp.float32)
     mixed = mixed + jnp.dot(

time: 469 us -> 447 us (0.953)
  waiting for transfers between devices: 395 us -> 362 us
  local copies, waits for them, and re-layouts: 5.52 us -> 11.5 us
  starting transfers between devices: 10.7 us -> 16.2 us
    ppermute x0 -> x3, waiting for transfers between devices: none -> 36.2 us  [rest_works(): jax.lax.ppermute(block_list[-1], along_axis, [(no, (no + 1) % world) for...]
    all_gather x1 -> x0, waiting for transfers between devices: 27.9 us -> none  [shards(): whole_up = lax.all_gather(upper, 'chan', axis=1, tiled=True)]
    all_gather x1, waiting for transfers between devices: 27.4 us -> 5.08 us  [shards(): whole_low = lax.all_gather(lower, 'chan', axis=1, tiled=True)]
    ppermute x4, waiting for transfers between devices: 27.7 us -> 13.5 us  [shifted(): lax.ppermute(value, axis, [(source, source + steps) for source in range(l...]
    unnamed x27 -> x30, local copies, waits for them, and re-layouts: 5.52 us -> 11.4 us
    all_gather x1, waiting for transfers between devices: 5.46 us -> 0.01 us  [shards(): whole = lax.all_gather(acted, 'chan', axis=1, tiled=True)]
  transfers between devices with their start and end apart: 12 -> 14, of which waited for: 12 -> 12; matrix products, arithmetic and copies ran while one was open for 6% -> 8% of each run, Pallas kernels for 0% -> 0%
where the time goes in v1:
time: 447 us
  waiting for transfers between devices  362 us (81%)
  matrix products  33.2 us (7%)
  starting transfers between devices  16.2 us (4%)
  between operations  14.3 us (3%)
  local copies, waits for them, and re-layouts  11.5 us (3%)
  other arithmetic  9.61 us (2%)
    reduce_scatter x1, waiting for transfers between devices, shards(): lax.psum_scatter(kernel, 'seq', scatter_dimension=1, tiled=True)  151 us
    all_gather x1, waiting for transfers between devices, shards(): all_blocks = lax.all_gather(block_partial_sums, 'seq', axis=0, tiled=True)  50.9 us
    reduce_scatter x1, waiting for transfers between devices, shards(): lax.psum_scatter(times_t(head_term, head_weight), 'chan', scatter_dimensi...  40.1 us
    ppermute x3, waiting for transfers between devices, rest_works(): jax.lax.ppermute(block_list[-1], along_axis, [(no, (no + 1) % world) for...  36.2 us
    reduce_scatter x1, waiting for transfers between devices, shards(): lax.psum_scatter(partial_value, 'chan', scatter_dimension=1, tiled=True)  34.6 us
    all_gather x1, waiting for transfers between devices, shards(): full_state = lax.all_gather(state, 'chan', axis=1, tiled=True)  29.2 us
    ppermute x4, waiting for transfers between devices, shifted(): lax.ppermute(value, axis, [(source, source + steps) for source in range(l...  13.5 us
    ppermute x4, starting transfers between devices, shifted(): lax.ppermute(value, axis, [(source, source + steps) for source in range(l...  11.6 us
  transfers between devices with their start and end apart: 14, of which 12 were waited for; matrix products, arithmetic and copies ran while one was open for 8% of the time, Pallas kernels for 0%

profile of v1, /device:TPU:2, one launch (start us, length us, event | category | flops | bytes accessed | tf_op | source)
XLA Modules:
  0.0 446.5 jit_solution(15942412659161946553)
XLA Ops:
  7.2 0.0 copy-start
  7.2 0.0 all-gather.8.cloned.1.call-start
  7.2 2.2 fusion.31
  9.4 0.0 all-gather.8.cloned.1.call-update
  9.4 0.0 all-gather.6.cloned.1.call-start
  9.5 1.3 collective-permute-start.1
  10.8 5.3 %collective-permute-start = (bf16[512,384]{1,0:T(8,128)(2,1)}, bf16[512,384]{1,0:T(8,128)(2,1)}, u32[]{:S(2)}, u32[]{:S(2)}) collective-permute-start(bf16[512,384]{1,0:T(8,128)(2,1)} %fusion.31), channel_id=1, source_target_pairs={{0,8},{4,12},{8,16},{12,20},{16,24},{20,28},{24,32},{28,36},{32,40... | collective-permute-start | bytes 1179656 | tf_op jit(solution)/shard_map/ppermute | solution.py:33
  16.1 6.5 %collective-permute-done.1 = bf16[512,384]{1,0:T(8,128)(2,1)S(1)} collective-permute-done((bf16[512,384]{1,0:T(8,128)(2,1)}, bf16[512,384]{1,0:T(8,128)(2,1)S(1)}, u32[]{:S(2)}, u32[]{:S(2)}) %collective-permute-start.1) | collective-permute-done | bytes 393248 | tf_op jit(solution)/shard_map/ppermute | solution.py:33
  22.6 1.5 collective-permute-start.2
  24.1 0.0 all-gather.6.cloned.1.call-update
  24.1 0.0 all-gather.10.cloned.1.call-start
  24.2 17.1 %collective-permute-done.2 = bf16[512,384]{1,0:T(8,128)(2,1)} collective-permute-done((bf16[512,384]{1,0:T(8,128)(2,1)S(1)}, bf16[512,384]{1,0:T(8,128)(2,1)}, u32[]{:S(2)}, u32[]{:S(2)}) %collective-permute-start.2) | collective-permute-done | bytes 393248 | tf_op jit(solution)/shard_map/ppermute | solution.py:16
  41.2 1.4 collective-permute-start.3
  42.6 11.3 %collective-permute-done.3 = bf16[512,384]{1,0:T(8,128)(2,1)} collective-permute-done((bf16[512,384]{1,0:T(8,128)(2,1)}, bf16[512,384]{1,0:T(8,128)(2,1)}, u32[]{:S(2)}, u32[]{:S(2)}) %collective-permute-start.3) | collective-permute-done | bytes 393248 | tf_op jit(solution)/shard_map/ppermute | solution.py:16
  54.0 1.5 collective-permute-start.4
  55.5 7.8 %collective-permute-done.4 = bf16[512,384]{1,0:T(8,128)(2,1)} collective-permute-done((bf16[512,384]{1,0:T(8,128)(2,1)}, bf16[512,384]{1,0:T(8,128)(2,1)}, u32[]{:S(2)}, u32[]{:S(2)}) %collective-permute-start.4) | collective-permute-done | bytes 393248 | tf_op jit(solution)/shard_map/ppermute | solution.py:16
  63.3 1.1 constant_dynamic-update-slice_fusion.7
  64.3 1.1 constant_dynamic-update-slice_fusion.6
  65.4 1.1 constant_dynamic-update-slice_fusion.5
  66.6 0.1 constant_dynamic-update-slice_fusion.4
  66.7 1.1 constant_dynamic-update-slice_fusion.3
  67.8 1.1 constant_dynamic-update-slice_fusion.2
  68.9 1.1 constant_dynamic-update-slice_fusion.1
  70.0 0.1 constant_dynamic-update-slice_fusion
  70.1 3.2 fusion.2
  73.3 3.7 fusion.11
  77.0 5.1 %all-gather.6.cloned.1.call-done = bf16[512,1536]{1,0:T(8,128)(2,1)} async-done(((bf16[512,384]{1,0:T(8,128)(2,1)}), bf16[512,1536]{1,0:T(8,128)(2,1)}) %all-gather.6.cloned.1.call-update) | async-done | bytes 1572880 | tf_op jit(solution)/shard_map/all_gather | solution.py:70
  82.1 3.9 fusion.5
  86.0 0.0 all-gather.10.cloned.1.call-update
  86.0 0.0 reduce-scatter.4.cloned.1.call-start
  86.1 29.2 %all-gather.10.cloned.1.call-done = bf16[512,1536]{1,0:T(8,128)(2,1)} async-done(((bf16[512,384]{1,0:T(8,128)(2,1)}), bf16[512,1536]{1,0:T(8,128)(2,1)}) %all-gather.10.cloned.1.call-update) | async-done | bytes 1572880 | tf_op jit(solution)/shard_map/all_gather | solution.py:79
  115.3 5.8 %convert_reduce_fusion = (f32[4,1024]{1,0:T(4,128)}, bf16[512,1024]{1,0:T(8,128)(2,1)}, f32[512,1024]{1,0:T(8,128)S(1)}) fusion(bf16[512,1536]{1,0:T(8,128)(2,1)} %all-gather.10.cloned.1.call-done, bf16[1536,1024]{1,0:T(8,128)(2,1)S(1)} %copy-done), kind=kOutput, calls=%fused_computation.8 | convolution fusion | flops 1615327232 | bytes 7880704 | tf_op jit(solution)/shard_map/dot_general | solution.py:80
  121.2 3.5 fusion.16
  124.6 0.0 reduce-scatter.4.cloned.1.call-update
  124.6 0.0 all-gather.12.cloned.1.call-start
  124.7 0.5 all-gather.12.cloned.1.call-update
  125.2 0.0 reduce-scatter.6.cloned.1.call-start
  125.3 40.1 %reduce-scatter.4.cloned.1.call-done = f32[512,384]{1,0:T(8,128)} async-done(((f32[512,1536]{1,0:T(8,128)}), f32[512,384]{1,0:T(8,128)}) %reduce-scatter.4.cloned.1.call-update) | async-done | bytes 786448 | tf_op jit(solution)/shard_map/reduce_scatter | solution.py:83
  165.3 1.3 convert_element_type.37
  166.7 3.5 collective-permute-start.6
  170.2 1.5 collective-permute-start.5
  171.7 2.3 fusion.9
  173.9 4.6 %collective-permute-done.6 = bf16[512,384]{1,0:T(8,128)(2,1)S(1)} collective-permute-done((bf16[512,384]{1,0:T(8,128)(2,1)S(1)}, bf16[512,384]{1,0:T(8,128)(2,1)S(1)}, u32[]{:S(2)}, u32[]{:S(2)}) %collective-permute-start.6) | collective-permute-done | bytes 393248 | tf_op jit(solution)/shard_map/ppermute | solution.py:33
  178.6 0.7 copy-done.6
  179.3 1.0 fusion.6
  180.3 2.4 collective-permute-done.5
  182.7 0.7 copy-done.4
  183.4 2.7 fusion
  186.2 0.0 reduce-scatter.6.cloned.1.call-update
  186.2 0.0 reduce-scatter.8.cloned.1.call-start
  186.2 0.0 copy-start.7
  186.3 2.6 convolution_bitcast_fusion.1
  188.9 1.0 convolution_bitcast_fusion
  189.9 1.0 convolution_bitcast_fusion.2
  190.9 3.3 pad_maximum_fusion
  194.3 0.0 reduce-scatter.8.cloned.1.call-update
  194.3 0.7 copy-done.8
  195.0 0.1 convert_reduce_fusion.1
  195.1 50.9 %all-gather.12.cloned.1.call-done = f32[64,4,1024]{2,1,0:T(4,128)} async-done(((f32[1,4,1024]{2,1,0:T(4,128)}), f32[64,4,1024]{2,1,0:T(4,128)}) %all-gather.12.cloned.1.call-update) | async-done | bytes 1048592 | tf_op jit(solution)/shard_map/all_gather | solution.py:107
  246.0 2.6 reshape.20
  248.5 2.4 convolution_multiply_fusion
  251.0 34.6 %reduce-scatter.6.cloned.1.call-done = f32[512,384]{1,0:T(8,128)} async-done(((f32[512,1536]{1,0:T(8,128)}), f32[512,384]{1,0:T(8,128)}) %reduce-scatter.6.cloned.1.call-update) | async-done | bytes 786448 | tf_op jit(solution)/shard_map/reduce_scatter | solution.py:95
  285.6 2.7 fusion.27
  288.3 151.3 %reduce-scatter.8.cloned.1.call-done = f32[3,24,384]{2,1,0:T(8,128)} async-done(((f32[3,1536,384]{2,1,0:T(8,128)}), f32[3,24,384]{2,1,0:T(8,128)}) %reduce-scatter.8.cloned.1.call-update) | async-done | bytes 110608 | tf_op jit(solution)/shard_map/reduce_scatter | solution.py:99
  (19 shorter events, 0.0 us)
Async XLA Ops:
  7.2 108.1 %copy-start = (bf16[1536,1024]{1,0:T(8,128)(2,1)S(1)}, bf16[1536,1024]{1,0:T(8,128)(2,1)}, u32[]{:S(2)}) copy-start(bf16[1536,1024]{1,0:T(8,128)(2,1)} %param.7) | copy-start | bytes 9437188
  7.2 66.1 %all-gather.8.cloned.1.call-start = ((), (), s32[]{:S(2)}) async-start(), calls=%async_computation.4 | async-start | bytes 1966080 | tf_op jit(solution)/shard_map/all_gather | solution.py:69
  9.4 72.6 %all-gather.6.cloned.1.call-start = ((), (), s32[]{:S(2)}) async-start(), calls=%async_computation.3 | async-start | bytes 1966080 | tf_op jit(solution)/shard_map/all_gather | solution.py:70
  9.5 13.1 %collective-permute-start.1 = (bf16[512,384]{1,0:T(8,128)(2,1)}, bf16[512,384]{1,0:T(8,128)(2,1)S(1)}, u32[]{:S(2)}, u32[]{:S(2)}) collective-permute-start(bf16[512,384]{1,0:T(8,128)(2,1)} %fusion.31), channel_id=1, source_target_pairs={{8,0},{12,4},{16,8},{20,12},{24,16},{28,20},{32,24},{36,28},{40,32... | collective-permute-start | bytes 1179656 | tf_op jit(solution)/shard_map/ppermute | solution.py:33
  10.8 13.3 %collective-permute-start = (bf16[512,384]{1,0:T(8,128)(2,1)}, bf16[512,384]{1,0:T(8,128)(2,1)}, u32[]{:S(2)}, u32[]{:S(2)}) collective-permute-start(bf16[512,384]{1,0:T(8,128)(2,1)} %fusion.31), channel_id=1, source_target_pairs={{0,8},{4,12},{8,16},{12,20},{16,24},{20,28},{24,32},{28,36},{32,40... | collective-permute-start | bytes 1179656 | tf_op jit(solution)/shard_map/ppermute | solution.py:33
  22.6 18.6 %collective-permute-start.2 = (bf16[512,384]{1,0:T(8,128)(2,1)S(1)}, bf16[512,384]{1,0:T(8,128)(2,1)}, u32[]{:S(2)}, u32[]{:S(2)}) collective-permute-start(bf16[512,384]{1,0:T(8,128)(2,1)S(1)} %collective-permute-done.1), channel_id=1, source_target_pairs={{0,1},{1,2},{2,3},{3,0},{4,5},{5,6},{6,7},{7,4},{8,9},{9,10},{10,1... | collective-permute-start | bytes 1179656 | tf_op jit(solution)/shard_map/ppermute | solution.py:16
  24.1 91.2 %all-gather.10.cloned.1.call-start = ((), (), s32[]{:S(2)}) async-start(), calls=%async_computation.5 | async-start | bytes 1966080 | tf_op jit(solution)/shard_map/all_gather | solution.py:79
  41.2 12.7 %collective-permute-start.3 = (bf16[512,384]{1,0:T(8,128)(2,1)}, bf16[512,384]{1,0:T(8,128)(2,1)}, u32[]{:S(2)}, u32[]{:S(2)}) collective-permute-start(bf16[512,384]{1,0:T(8,128)(2,1)} %collective-permute-done.2), channel_id=1, source_target_pairs={{0,1},{1,2},{2,3},{3,0},{4,5},{5,6},{6,7},{7,4},{8,9},{9,10},{10,1... | collective-permute-start | bytes 1179656 | tf_op jit(solution)/shard_map/ppermute | solution.py:16
  54.0 9.3 %collective-permute-start.4 = (bf16[512,384]{1,0:T(8,128)(2,1)}, bf16[512,384]{1,0:T(8,128)(2,1)}, u32[]{:S(2)}, u32[]{:S(2)}) collective-permute-start(bf16[512,384]{1,0:T(8,128)(2,1)} %collective-permute-done.3), channel_id=1, source_target_pairs={{0,1},{1,2},{2,3},{3,0},{4,5},{5,6},{6,7},{7,4},{8,9},{9,10},{10,1... | collective-permute-start | bytes 1179656 | tf_op jit(solution)/shard_map/ppermute | solution.py:16
  73.3 8.8 %copy-start.2 = (bf16[512,384]{1,0:T(8,128)(2,1)S(1)}, bf16[512,384]{1,0:T(8,128)(2,1)}, u32[]{:S(2)}) copy-start(bf16[512,384]{1,0:T(8,128)(2,1)} %param.5) | copy-start | bytes 1179652
  86.0 79.3 %reduce-scatter.4.cloned.1.call-start = ((), (), s32[]{:S(2)}) async-start(), calls=%async_computation.6 | async-start | bytes 3932160 | tf_op jit(solution)/shard_map/reduce_scatter | solution.py:83
  115.3 5.8 %copy-start.10 = (bf16[512,1024]{1,0:T(8,128)(2,1)S(1)}, bf16[512,1024]{1,0:T(8,128)(2,1)}, u32[]{:S(2)}) copy-start(bf16[512,1024]{1,0:T(8,128)(2,1)} %param.8) | copy-start | bytes 3145732
  124.6 121.3 %all-gather.12.cloned.1.call-start = ((), (), s32[]{:S(2)}) async-start(), calls=%async_computation.9 | async-start | bytes 1064960 | tf_op jit(solution)/shard_map/all_gather | solution.py:107
  125.2 160.4 %reduce-scatter.6.cloned.1.call-start = ((), (), s32[]{:S(2)}) async-start(), calls=%async_computation.7 | async-start | bytes 3932160 | tf_op jit(solution)/shard_map/reduce_scatter | solution.py:95
  165.3 14.0 %copy-start.1 = (bf16[1,3,1536,384]{3,2,1,0:T(8,128)(2,1)S(1)}, bf16[1,3,1536,384]{3,2,1,0:T(8,128)(2,1)}, u32[]{:S(2)}) copy-start(bf16[1,3,1536,384]{3,2,1,0:T(8,128)(2,1)} %param.6) | copy-start | bytes 10616836
  166.7 13.7 %copy-start.3 = (bf16[512,384]{1,0:T(8,128)(2,1)}, bf16[512,384]{1,0:T(8,128)(2,1)S(1)}, u32[]{:S(2)}) copy-start(bf16[512,384]{1,0:T(8,128)(2,1)S(1)} %convert_element_type.37) | copy-start | bytes 1179652
  166.7 11.9 %collective-permute-start.6 = (bf16[512,384]{1,0:T(8,128)(2,1)S(1)}, bf16[512,384]{1,0:T(8,128)(2,1)S(1)}, u32[]{:S(2)}, u32[]{:S(2)}) collective-permute-start(bf16[512,384]{1,0:T(8,128)(2,1)S(1)} %convert_element_type.37), channel_id=1, source_target_pairs={{0,8},{4,12},{8,16},{12,20},{16,24},{20,28},{24,32},{28,36},{32,40... | collective-permute-start | bytes 1179656 | tf_op jit(solution)/shard_map/ppermute | solution.py:33
  170.2 12.5 %collective-permute-start.5 = (bf16[512,384]{1,0:T(8,128)(2,1)S(1)}, bf16[512,384]{1,0:T(8,128)(2,1)S(1)}, u32[]{:S(2)}, u32[]{:S(2)}) collective-permute-start(bf16[512,384]{1,0:T(8,128)(2,1)S(1)} %convert_element_type.37), channel_id=1, source_target_pairs={{8,0},{12,4},{16,8},{20,12},{24,16},{28,20},{32,24},{36,28},{40,32... | collective-permute-start | bytes 1179656 | tf_op jit(solution)/shard_map/ppermute | solution.py:33
  178.6 0.7 copy-start.6
  182.7 0.7 copy-start.4
  186.2 253.5 %reduce-scatter.8.cloned.1.call-start = ((), (), s32[]{:S(2)}) async-start(), calls=%async_computation.8 | async-start | bytes 7188480 | tf_op jit(solution)/shard_map/reduce_scatter | solution.py:99
  186.2 2.6 copy-start.7
  186.3 2.6 copy-start.9
  188.9 1.0 copy-start.5
  194.3 0.7 copy-start.8
Sparse Core Ops, SparseCore 0:
  10.4 40.3 all-gather.7
  52.6 29.3 all-gather.5
  86.1 29.1 all-gather.9
  124.8 40.5 reduce-scatter.3
  168.5 77.3 all-gather.11
  248.4 37.2 reduce-scatter.5
  290.5 149.1 reduce-scatter.7
